TPU v7x, 32 devices: a whole 2x2x4 slice. The times are simulated.
32 devices in a mesh: dp: 16 (over z, y, core), tensor: 2 (over x).
Axes of the slice: x: 2, y: 2, z: 4, core: 2. Of those that a mesh axis runs over, the one named last changes fastest.
Arguments:
- output_gradient: bfloat16 [6144, 8192], P(('dp', 'tensor')), may hold values from -6 to 6
- attention_input: bfloat16 [6144, 8192], P('dp', 'tensor'), may hold values from -6 to 6
- projection_weight: bfloat16 [8192, 8192], P('tensor', 'dp'), may hold values from -0.0625 to 0.0625
- adapter_down: float32 [16, 8192, 64], P('dp', 'tensor'), may hold values from -0.0625 to 0.0625
- adapter_up: float32 [16, 64, 8192], P('dp', None, 'tensor'), may hold values from -0.0625 to 0.0625
- down_first_moment: float32 [16, 8192, 64], P('dp', 'tensor'), may hold values from -0.75 to 0.75
- down_second_moment: float32 [16, 8192, 64], P('dp', 'tensor'), may hold values from 0.001 to 0.01
- up_first_moment: float32 [16, 64, 8192], P('dp', None, 'tensor'), may hold values from -0.75 to 0.75
- up_second_moment: float32 [16, 64, 8192], P('dp', None, 'tensor'), may hold values from 0.001 to 0.01
- tenant_lookup: int32 [16], replicated, may hold values from 0 to 3, never falling along the last dimension, each value on 1 to 13 neighbouring positions
- active_token_rows: int32 [16], P('dp'), may hold values from 128 to 384, as said below
Outputs:
- input_gradient: bfloat16 [6144, 8192], P('dp', 'tensor')
- fresh_adapter_down: float32 [16, 8192, 64], P('dp', 'tensor')
- fresh_down_first_moment: float32 [16, 8192, 64], P('dp', 'tensor')
- fresh_down_second_moment: float32 [16, 8192, 64], P('dp', 'tensor')
- fresh_adapter_up: float32 [16, 64, 8192], P('dp', None, 'tensor')
- fresh_up_first_moment: float32 [16, 64, 8192], P('dp', None, 'tensor')
- fresh_up_second_moment: float32 [16, 64, 8192], P('dp', None, 'tensor')
Inputs may be any that keep to these rules, and one draw needn't show every extreme that they name: `tenant_lookup`: tenants own contiguous runs of dp indices, numbered in order; every tenant owns at least one index and the largest owns 16 - 3. `active_token_rows`: multiples of 128; some dp index has all 384 slots live.
All inputs are finite; a program needn't handle non-finite values.
Results may differ from a plain program's by a relative error of at most 0.0037.
Values may be sent and summed in bfloat16 or wider, within the bound.
A program may use at most 256 MiB of HBM per device.

v0:
```python
import jax
import jax.numpy as jnp
from jax import lax
from jax.sharding import PartitionSpec as P

TENANTS = 4
ADAM_STEP = 10


adapter_scale = 2.0
beta_one = 0.9
beta_two = 0.999
learn_rate = 0.02
adam_eps = 1e-08


def apply_adam_rule(param, grad, moment, second):
    new_moment = beta_one * moment + (1.0 - beta_one) * grad
    new_second = beta_two * second + (1.0 - beta_two) * grad * grad
    fix_one = 1.0 - beta_one**ADAM_STEP
    fix_two = 1.0 - beta_two**ADAM_STEP
    step_size = new_moment / fix_one / (jnp.sqrt(new_second / fix_two) + adam_eps)
    return (param - learn_rate * step_size, new_moment, new_second)


def contract_trailing(left, right):
    return lax.dot_general(
        left, right, (((1,), (1,)), ((), ())), preferred_element_type=jnp.float32
    )


def contract_leading(left, right):
    return lax.dot_general(
        left, right, (((0,), (0,)), ((), ())), preferred_element_type=jnp.float32
    )


def on_device(
    output_gradient,
    attention_input,
    projection_weight,
    adapter_down,
    adapter_up,
    down_first_moment,
    down_second_moment,
    up_first_moment,
    up_second_moment,
    tenant_lookup,
    active_token_rows,
):
    tensor_pos = lax.axis_index("tensor")
    dp_pos = lax.axis_index("dp")
    shard_rows = output_gradient.shape[0]
    columns = attention_input.shape[1]
    positions = tensor_pos * shard_rows + jnp.arange(shard_rows, dtype=jnp.int32)
    masked = jnp.where(
        (positions < active_token_rows[0])[:, None],
        output_gradient,
        jnp.zeros_like(output_gradient),
    )
    down_portion = adapter_down[0].astype(jnp.bfloat16)
    up_portion = adapter_up[0].astype(jnp.bfloat16)
    gathered = lax.all_gather(masked, "tensor", axis=0, tiled=True)
    frozen_gradient = contract_trailing(
        gathered, lax.all_gather(projection_weight, "dp", axis=1, tiled=True)
    )
    tenant_match_mask = lax.dynamic_slice_in_dim(gathered, tensor_pos * columns, columns, 1)
    in_part = jnp.dot(attention_input, down_portion, preferred_element_type=jnp.float32)
    grad_part = contract_trailing(tenant_match_mask, up_portion)
    rank_space_input, rank_space_gradient = lax.psum((in_part, grad_part), "tensor")
    rank_space_input = rank_space_input.astype(jnp.bfloat16)
    rank_space_gradient = rank_space_gradient.astype(jnp.bfloat16)
    input_gradient = (
        frozen_gradient + adapter_scale * contract_trailing(rank_space_gradient, down_portion)
    ).astype(jnp.bfloat16)
    down_partial = adapter_scale * contract_leading(attention_input, rank_space_gradient)
    up_partial = adapter_scale * contract_leading(rank_space_input, tenant_match_mask)
    live_count = active_token_rows[0].astype(jnp.float32)
    own_tenant = tenant_lookup[dp_pos]
    slots = (jnp.arange(TENANTS, dtype=jnp.int32) == own_tenant).astype(jnp.float32)
    slot_a = slots[:, None, None] * down_partial[None]
    slot_b = slots[:, None, None] * up_partial[None]
    slot_count = slots * live_count
    total_a, total_b, total_count = lax.psum((slot_a, slot_b, slot_count), "dp")
    sum_a = lax.dynamic_index_in_dim(total_a, own_tenant, 0, keepdims=False)
    sum_b = lax.dynamic_index_in_dim(total_b, own_tenant, 0, keepdims=False)
    count = lax.dynamic_index_in_dim(total_count, own_tenant, 0, keepdims=False)
    down_gradient = sum_a / count
    up_gradient = sum_b / count
    fresh_adapter_down, fresh_down_first_moment, fresh_down_second_moment = apply_adam_rule(
        adapter_down[0], down_gradient, down_first_moment[0], down_second_moment[0]
    )
    fresh_adapter_up, fresh_up_first_moment, fresh_up_second_moment = apply_adam_rule(
        adapter_up[0], up_gradient, up_first_moment[0], up_second_moment[0]
    )
    return (
        input_gradient,
        fresh_adapter_down[None],
        fresh_down_first_moment[None],
        fresh_down_second_moment[None],
        fresh_adapter_up[None],
        fresh_up_first_moment[None],
        fresh_up_second_moment[None],
    )


def solution(mesh):
    return jax.shard_map(
        on_device,
        mesh=mesh,
        in_specs=(
            P(("dp", "tensor"), None),
            P("dp", "tensor"),
            P("tensor", "dp"),
            P("dp", "tensor", None),
            P("dp", None, "tensor"),
            P("dp", "tensor", None),
            P("dp", "tensor", None),
            P("dp", None, "tensor"),
            P("dp", None, "tensor"),
            P(),
            P("dp"),
        ),
        out_specs=(
            P("dp", "tensor"),
            P("dp", "tensor", None),
            P("dp", "tensor", None),
            P("dp", "tensor", None),
            P("dp", None, "tensor"),
            P("dp", None, "tensor"),
            P("dp", None, "tensor"),
        ),
        check_vma=False,
    )
```

profile of v0, /device:TPU:0, one launch (start us, length us, event | category | flops | bytes accessed | tf_op | source)
XLA Modules:
  0.0 667.0 jit_solution(10896862889923557850)
XLA Ops:
  8.0 3.9 broadcast_select_fusion
  12.0 0.0 all-reduce.5.cloned.1.call-start
  12.1 2.2 fusion.6
  14.3 0.6 dynamic_slice.19
  14.8 0.6 compare_convert_fusion
  15.5 79.7 %all-gather.3.cloned.1.call-done = bf16[384,8192]{1,0:T(8,128)(2,1)} async-done(((bf16[192,8192]{1,0:T(8,128)(2,1)}), bf16[384,8192]{1,0:T(8,128)(2,1)}) %all-gather.3.cloned.1.call-update) | async-done | bytes 6291472 | tf_op jit(solution)/shard_map/all_gather | solution.py:63
  95.2 3.3 fusion.2
  98.5 11.5 %all-reduce.6 = (bf16[384,64]{0,1:T(8,128)(2,1)S(1)}, bf16[384,64]{1,0:T(8,128)(2,1)}) all-reduce(f32[384,64]{0,1:T(8,128)S(1)} %fusion.2, f32[384,64]{1,0:T(8,128)S(1)} %fusion.6), channel_id=1, replica_groups=mesh['dp'=16,'tensor'=2] {'tensor'}, use_global_device_ids=true, to_apply=%region_0.1 | all-reduce | flops 49152 | bytes 294912 | tf_op jit(solution)/shard_map/psum | solution.py:70
  110.0 0.7 fusion
  110.7 2.7 broadcast_multiply_fusion.1
  113.4 0.8 copy-done.1
  114.2 0.7 convolution_multiply_fusion
  114.9 2.6 broadcast_multiply_fusion
  117.5 0.0 all-gather.5.cloned.1.call-start
  117.6 0.7 all-gather.5.cloned.1.call-update
  118.3 0.7 compare_select_fusion
  118.9 32.9 %psum.37 = f32[4]{0:T(128)S(1)} all-reduce(f32[4]{0:T(128)S(1)} %compare_select_fusion), channel_id=1, replica_groups=mesh['dp'=16,'tensor'=2] {'dp'}, use_global_device_ids=true, to_apply=%region_2.3 | all-reduce | flops 4 | bytes 32 | tf_op jit(solution)/shard_map/psum | solution.py:84
  153.7 0.6 dynamic_slice.21
  154.3 135.1 %all-reduce.5.cloned.1.call-done = (f32[4,4096,64]{1,2,0:T(8,128)}, f32[4,64,4096]{2,1,0:T(8,128)}) async-done(((f32[4,4096,64]{1,2,0:T(8,128)}, f32[4,64,4096]{2,1,0:T(8,128)}), (f32[4,4096,64]{1,2,0:T(8,128)}, f32[4,64,4096]{2,1,0:T(8,128)})) %all-reduce.5.cloned.1.call-update) | async-done | bytes 8388624 | tf_op jit(solution)/shard_map/psum | solution.py:84
  289.4 5.3 multiply_subtract_fusion.1
  294.7 4.2 multiply_subtract_fusion
  298.9 318.1 %all-gather.5.cloned.1.call-done = bf16[4096,8192]{1,0:T(8,128)(2,1)} async-done(((bf16[4096,512]{1,0:T(8,128)(2,1)}), bf16[4096,8192]{1,0:T(8,128)(2,1)}) %all-gather.5.cloned.1.call-update) | async-done | bytes 67108880 | tf_op jit(solution)/shard_map/all_gather | solution.py:65
  617.0 37.7 %fusion.20 = f32[384,4096]{1,0:T(8,128)} fusion(bf16[384,8192]{1,0:T(8,128)(2,1)} %all-gather.3.cloned.1.call-done, bf16[4096,8192]{1,0:T(8,128)(2,1)} %all-gather.5.cloned.1.call-done), kind=kOutput, calls=%fused_computation.35 | convolution fusion | flops 25769803776 | bytes 79691776 | tf_op jit(solution)/shard_map/dot_general | solution.py:27
  654.7 5.8 add_convert_fusion
  (17 shorter events, 0.1 us)
Async XLA Ops:
  7.2 4.9 copy-start
  7.2 88.0 %all-gather.3.cloned.1.call-start = ((), (), s32[]{:S(2)}) async-start(), calls=%async_computation | async-start | bytes 9437184 | tf_op jit(solution)/shard_map/all_gather | solution.py:63
  12.0 2.3 copy-start.6
  12.0 277.4 %all-reduce.5.cloned.1.call-start = ((), (), s32[]{:S(2)}) async-start(), calls=%async_computation.2 | async-start | bytes 16777216 | tf_op jit(solution)/shard_map/psum | solution.py:84
  110.0 4.2 copy-start.1
  110.0 4.2 copy-start.5
  117.5 499.5 %all-gather.5.cloned.1.call-start = ((), (), s32[]{:S(2)}) async-start(), calls=%async_computation.1 | async-start | bytes 71303168 | tf_op jit(solution)/shard_map/all_gather | solution.py:65
  289.4 5.3 copy-start.2
  289.4 5.3 copy-start.3
  289.4 5.3 copy-start.4
Sparse Core Ops, SparseCore 0:
  12.1 83.0 all-gather.2
  117.6 171.6 all-reduce.4
  291.0 325.9 all-gather.4
where the time goes:
time: 667 us
  waiting for transfers between devices  534 us (80%)
  matrix products  50.3 us (8%)
  blocking collectives  44.4 us (7%)
  other arithmetic  20 us (3%)
  between operations  16.6 us (2%)
    all_gather x1, waiting for transfers between devices, on_device(): lax.all_gather(projection_weight, 'dp', axis=1, tiled=True)  318 us
    psum x1, waiting for transfers between devices, on_device(): total_a, total_b, total_count = lax.psum((slot_a, slot_b, slot_count), 'dp')  135 us
    all_gather x1, waiting for transfers between devices, on_device(): gathered = lax.all_gather(masked, 'tensor', axis=0, tiled=True)  79.7 us
    dot_general x3, matrix products, contract_trailing(): lax.dot_general(left, right, (((1,), (1,)), ((), ())), preferred_element_...  46.8 us
    psum x1, blocking collectives, on_device(): total_a, total_b, total_count = lax.psum((slot_a, slot_b, slot_count), 'dp')  32.9 us
  transfers between devices with their start and end apart: 3, of which 3 were waited for; matrix products, arithmetic and copies ran while one was open for 2% of the time, Pallas kernels for 0%

commit v1 on v0

--- a/solution.py
+++ b/solution.py
@@ -1,6 +1,8 @@
 import jax
 import jax.numpy as jnp
 from jax import lax
+from jax.experimental import pallas as pl
+from jax.experimental.pallas import tpu as pltpu
 from jax.sharding import PartitionSpec as P
 
 TENANTS = 4
@@ -104,9 +106,537 @@
     )
 
 
+MESH = pl.DeviceIdType.MESH
+CHUNKS = 16
+LOW_STEP = 6
+OUT_STEP = 7
+EXTRA = 8
+
+
+def fused_kernel(
+    g, attn, w, a_half, b_half, lookup, live,
+    out, sums,
+    wbuf, gk, gx, attn_v, precv, psend, acc, low_out, low_in_buf, lin, lgr, part, lay,
+    up_in, down_in, up_out, down_out,
+    local_sem, w_send, w_recv, g_send, g_recv, p_send, p_recv, o_sem, lr_sem,
+    part_send, part_recv, chain_send, chain_recv, fin_send, fin_recv,
+):
+    dp = lax.axis_index("dp")
+    x = lax.axis_index("tensor")
+    z, y, c = dp // 4, (dp // 2) % 2, dp % 2
+    me = dp % 4
+    rows, width = g.shape
+    both = 2 * rows
+    columns, kblk = w.shape
+    cn = columns // CHUNKS
+    span = 2 * kblk
+    half = width // 2
+    piece = columns // 4
+    rank = b_half.shape[0]
+
+    here = {"dp": dp, "tensor": x}
+    across = {"dp": dp, "tensor": 1 - x}
+    y_dp = z * 4 + (1 - y) * 2 + c
+    y_peer = {"dp": y_dp, "tensor": x}
+    diag = {"dp": y_dp, "tensor": 1 - x}
+    sibling = {"dp": dp - c + (1 - c), "tensor": x}
+    corner = {"dp": z * 4 + (1 - y) * 2 + (1 - c), "tensor": x}
+    above = {"dp": lax.rem(dp + 4, 16), "tensor": x}
+    below = {"dp": lax.rem(dp + 12, 16), "tensor": x}
+
+    barrier = pltpu.get_barrier_semaphore()
+    for other in (across, y_peer, diag, sibling, corner):
+        pl.semaphore_signal(barrier, inc=1, device_id=other, device_id_type=MESH)
+
+    @pl.when(z < 3)
+    def _():
+        pl.semaphore_signal(barrier, inc=1, device_id=above, device_id_type=MESH)
+
+    @pl.when(z > 0)
+    def _():
+        pl.semaphore_signal(barrier, inc=1, device_id=below, device_id_type=MESH)
+
+    pl.semaphore_wait(barrier, 5 + (z < 3).astype(jnp.int32) + (z > 0).astype(jnp.int32))
+
+    def remote(src, dst, send, recv, where):
+        return pltpu.make_async_remote_copy(
+            src_ref=src, dst_ref=dst, send_sem=send, recv_sem=recv,
+            device_id=where, device_id_type=MESH,
+        )
+
+    def w_slot(layer, core, n):
+        return wbuf.at[
+            pl.ds(pl.multiple_of(n * cn, cn), cn),
+            pl.ds(pl.multiple_of(layer * span + core * kblk, kblk), kblk),
+        ]
+
+    def w_copy(layer, n, way):
+        slot = w_slot(layer, c, n)
+        where = (above, below, sibling)[way]
+        return remote(
+            slot, slot, w_send.at[layer, way, n], w_recv.at[layer, way // 2, n], where
+        )
+
+    def own_copy(n, way):
+        where = (above, below, sibling)[way]
+        return remote(
+            w.at[pl.ds(pl.multiple_of(n * cn, cn), cn), :], w_slot(z, c, n),
+            w_send.at[z, way, n], w_recv.at[z, way // 2, n], where,
+        )
+
+    def own_start(n):
+        @pl.when(z < 3)
+        def _():
+            own_copy(n, 0).start()
+
+        @pl.when(z > 0)
+        def _():
+            own_copy(n, 1).start()
+
+        own_copy(n, 2).start()
+
+    def w_wait(layer, core, way, n):
+        slot = w_slot(layer, core, n)
+        remote(slot, slot, w_send.at[layer, 2, n], w_recv.at[layer, way, n], sibling).wait_recv()
+
+    def relay(dist, n):
+        @pl.when(z >= dist)
+        def _():
+            w_wait(z - dist, c, 0, n)
+
+            @pl.when(z < 3)
+            def _():
+                w_copy(z - dist, n, 0).start()
+
+            w_copy(z - dist, n, 2).start()
+
+        @pl.when(z + dist <= 3)
+        def _():
+            w_wait(z + dist, c, 0, n)
+
+            @pl.when(z > 0)
+            def _():
+                w_copy(z + dist, n, 1).start()
+
+            w_copy(z + dist, n, 2).start()
+
+    mine = pl.ds(pl.multiple_of(x * rows, rows), rows)
+    theirs = pl.ds(pl.multiple_of(both + x * rows, rows), rows)
+
+    def g_cols(layer, line):
+        return g.at[:, pl.ds(pl.multiple_of(layer * 2 * span + line * span, span), span)]
+
+    def g_copies():
+        copies = [
+            remote(
+                g.at[:, pl.ds(pl.multiple_of((1 - x) * half, half), half)],
+                gx.at[mine, :], g_send.at[12], g_recv.at[12], across,
+            )
+        ]
+        for k in range(4):
+            cols = pl.ds(k * span, span)
+            copies.append(remote(g_cols(k, y), gk.at[mine, cols], g_send.at[k], g_recv.at[k], across))
+            copies.append(remote(g_cols(k, 1 - y), gk.at[theirs, cols], g_send.at[4 + k], g_recv.at[4 + k], y_peer))
+            copies.append(remote(g_cols(k, 1 - y), gk.at[theirs, cols], g_send.at[8 + k], g_recv.at[8 + k], diag))
+        return copies
+
+    def g_arrivals():
+        row_x = pl.ds(pl.multiple_of((1 - x) * rows, rows), rows)
+        row_y = pl.ds(pl.multiple_of(both + x * rows, rows), rows)
+        row_d = pl.ds(pl.multiple_of(both + (1 - x) * rows, rows), rows)
+        remote(gx.at[row_x, :], gx.at[row_x, :], g_send.at[12], g_recv.at[12], across).wait_recv()
+        for k in range(4):
+            cols = pl.ds(k * span, span)
+            for base, where in ((0, row_x), (4, row_y), (8, row_d)):
+                spot = gk.at[where, cols]
+                remote(spot, spot, g_send.at[base + k], g_recv.at[base + k], across).wait_recv()
+
+    def local_copies():
+        copies = [
+            pltpu.make_async_copy(attn, attn_v, local_sem.at[0]),
+            pltpu.make_async_copy(
+                w, wbuf.at[:, pl.ds(pl.multiple_of(z * span + c * kblk, kblk), kblk)], local_sem.at[1]
+            ),
+            pltpu.make_async_copy(
+                g.at[:, pl.ds(pl.multiple_of(x * half, half), half)], gx.at[mine, :], local_sem.at[2]
+            ),
+        ]
+        for k in range(4):
+            copies.append(pltpu.make_async_copy(
+                g_cols(k, y), gk.at[mine, pl.ds(k * span, span)], local_sem.at[3 + k]
+            ))
+        return copies
+
+    own_start(0)
+    for copy in g_copies():
+        copy.start()
+    for copy in local_copies():
+        copy.start()
+
+    keep = lax.broadcasted_iota(jnp.int32, (both, 1), 0) < live[0]
+
+    def low_copy():
+        return remote(low_out, low_in_buf, lr_sem.at[0], lr_sem.at[1], across)
+
+    def low_first():
+        for copy in local_copies():
+            copy.wait()
+        g_arrivals()
+        low_out[:, :rank] = jnp.dot(attn_v[...], a_half[...], preferred_element_type=jnp.float32)
+        low_out[:, rank:] = contract_trailing(gx[...], b_half[...])
+        low_copy().start()
+
+    mates = [
+        {"dp": z * 4 + q, "tensor": x} for q in range(4)
+    ]
+
+    def part_copy(q):
+        return remote(part.at[q], lay.at[me], part_send.at[q], part_recv.at[me], mates[q])
+
+    def low_second():
+        low_copy().wait()
+        total = low_out[...] + low_in_buf[...]
+        low_in = total[:, :rank].astype(jnp.bfloat16)
+        low_grad = total[:, rank:].astype(jnp.bfloat16)
+        zero = jnp.zeros_like(low_in)
+        lin[...] = jnp.where(keep, low_in, zero)
+        lgr[...] = jnp.where(keep, low_grad, zero)
+        for q in range(4):
+            cols = pl.ds(q * piece, piece)
+            part[q, :rank, :] = adapter_scale * contract_leading(lgr[...], attn_v[:, cols])
+            part[q, rank : 2 * rank, :] = adapter_scale * contract_leading(lin[...], gx[:, cols])
+            part[q, 2 * rank :, :] = jnp.full((EXTRA, piece), live[0].astype(jnp.float32))
+            copy = part_copy(q)
+
+            @pl.when(q != me)
+            def _(copy=copy):
+                copy.start()
+
+    def parts_in():
+        for q in range(4):
+            @pl.when(q != me)
+            def _(q=q):
+                remote(lay.at[q], lay.at[q], part_send.at[q], part_recv.at[q], sibling).wait_recv()
+
+            @pl.when(q == me)
+            def _(q=q):
+                lay[q] = part[q]
+
+    tall = 2 * rank + EXTRA
+
+    def tenant(i):
+        return lookup[i]
+
+    def sum_of(who, where):
+        total = None
+        for q in range(4):
+            term = jnp.where(tenant(z * 4 + q) == who, lay[q, where, :], 0.0)
+            total = term if total is None else total + term
+        return total
+
+    low_nb = jnp.maximum(z * 4 - 1, 0)
+    high_nb = jnp.minimum(z * 4 + 4, 15)
+
+    def chain_copy(way):
+        if way == 0:
+            return remote(up_out, up_in, chain_send.at[0], chain_recv.at[0], above)
+        return remote(down_out, down_in, chain_send.at[1], chain_recv.at[1], below)
+
+    def go_up():
+        who = tenant(z * 4 + 3)
+
+        @pl.when(z > 0)
+        def _():
+            remote(up_in, up_in, chain_send.at[0], chain_recv.at[0], below).wait_recv()
+
+        @pl.when(z == 0)
+        def _():
+            up_in[...] = jnp.zeros_like(up_in)
+
+        def body(i, _):
+            where = pl.ds(pl.multiple_of(i * 8, 8), 8)
+            joined = jnp.where(tenant(low_nb) == who, up_in[where, :], 0.0)
+            up_out[where, :] = sum_of(who, where) + joined
+            return 0
+
+        lax.fori_loop(0, tall // 8, body, 0)
+
+        @pl.when(z < 3)
+        def _():
+            chain_copy(0).start()
+
+    def go_down():
+        who = tenant(z * 4)
+
+        @pl.when(z < 3)
+        def _():
+            remote(down_in, down_in, chain_send.at[1], chain_recv.at[1], above).wait_recv()
+
+        @pl.when(z == 3)
+        def _():
+            down_in[...] = jnp.zeros_like(down_in)
+
+        def body(i, _):
+            where = pl.ds(pl.multiple_of(i * 8, 8), 8)
+            joined = jnp.where(tenant(high_nb) == who, down_in[where, :], 0.0)
+            down_out[where, :] = sum_of(who, where) + joined
+            return 0
+
+        lax.fori_loop(0, tall // 8, body, 0)
+
+        @pl.when(z > 0)
+        def _():
+            chain_copy(1).start()
+
+    def fin_copy(q):
+        return remote(lay.at[q], sums.at[me], fin_send.at[q], fin_recv.at[me], mates[q])
+
+    def own_sum(q):
+        return pltpu.make_async_copy(lay.at[q], sums.at[q], local_sem.at[7])
+
+    def totals():
+        def body(i, _):
+            where = pl.ds(pl.multiple_of(i * 8, 8), 8)
+            old = [lay[q, where, :] for q in range(4)]
+            lower, upper = up_in[where, :], down_in[where, :]
+            for q in range(4):
+                who = tenant(z * 4 + q)
+                total = jnp.where(tenant(low_nb) == who, lower, 0.0)
+                total = total + jnp.where(tenant(high_nb) == who, upper, 0.0)
+                for k in range(4):
+                    total = total + jnp.where(tenant(z * 4 + k) == who, old[k], 0.0)
+                lay[q, where, :] = total
+            return 0
+
+        lax.fori_loop(0, tall // 8, body, 0)
+        for q in range(4):
+            @pl.when(q != me)
+            def _(q=q):
+                fin_copy(q).start()
+
+            @pl.when(q == me)
+            def _(q=q):
+                own_sum(q).start()
+
+    slots = psend.shape[0]
+
+    def p_copy(n):
+        return remote(
+            psend.at[n % slots], precv.at[n], p_send.at[n], p_recv.at[n], y_peer
+        )
+
+    def product(n, _):
+        for k in range(4):
+            w_wait(k, 1 - c, 1, n)
+
+        @pl.when(n >= slots)
+        def _():
+            p_copy(n - slots).wait_send()
+
+        block = wbuf[pl.ds(pl.multiple_of(n * cn, cn), cn), :]
+        acc[n % slots] = contract_trailing(gk[:both, :], block)
+        psend[n % slots] = contract_trailing(gk[both:, :], block).astype(jnp.bfloat16)
+        p_copy(n).start()
+        return 0
+
+    def o_copy(n):
+        return pltpu.make_async_copy(
+            precv.at[n], out.at[:, pl.ds(pl.multiple_of(n * cn, cn), cn)], o_sem.at[n]
+        )
+
+    def finish(n, _):
+        remote(precv.at[n], precv.at[n], p_send.at[n], p_recv.at[n], y_peer).wait_recv()
+        low = contract_trailing(lgr[...], a_half[pl.ds(pl.multiple_of(n * cn, cn), cn), :])
+        total = acc[n % slots] + precv[n].astype(jnp.float32) + adapter_scale * low
+        precv[n] = jnp.where(keep, total, 0.0).astype(jnp.bfloat16)
+        o_copy(n).start()
+        return 0
+
+    def done(s):
+        goal = jnp.minimum(2 * (s - OUT_STEP + 1), s - 2)
+        return jnp.clip(goal, 0, CHUNKS)
+
+    def step(s, _):
+        @pl.when(s + 1 < CHUNKS)
+        def _():
+            own_start(s + 1)
+
+        for dist in (1, 2, 3):
+            n = s - (dist - 1)
+
+            @pl.when((n >= 0) & (n < CHUNKS))
+            def _(dist=dist, n=n):
+                relay(dist, n)
+
+        @pl.when(s == LOW_STEP)
+        def _():
+            low_first()
+
+        @pl.when(s == LOW_STEP + 1)
+        def _():
+            low_second()
+
+        @pl.when(s == LOW_STEP + 2)
+        def _():
+            parts_in()
+
+        @pl.when(s == LOW_STEP + 2 + z)
+        def _():
+            go_up()
+
+        @pl.when(s == LOW_STEP + 5 - z)
+        def _():
+            go_down()
+
+        @pl.when(s == LOW_STEP + 6)
+        def _():
+            totals()
+
+        lax.fori_loop(done(s - 1), done(s), product, 0)
+        lax.fori_loop(done(s - 2), done(s - 1), finish, 0)
+        return 0
+
+    lax.fori_loop(0, CHUNKS + 4, step, 0)
+
+    for copy in g_copies():
+        copy.wait_send()
+    for q in range(4):
+        @pl.when(q != me)
+        def _(q=q):
+            part_copy(q).wait_send()
+            fin_copy(q).wait_send()
+            remote(lay.at[q], sums.at[q], fin_send.at[q], fin_recv.at[q], sibling).wait_recv()
+
+        @pl.when(q == me)
+        def _(q=q):
+            own_sum(q).wait()
+
+    @pl.when(z < 3)
+    def _():
+        chain_copy(0).wait_send()
+
+    @pl.when(z > 0)
+    def _():
+        chain_copy(1).wait_send()
+
+    def drain(n, _):
+        o_copy(n).wait()
+
+        @pl.when(n >= CHUNKS - slots)
+        def _():
+            p_copy(n).wait_send()
+
+        for k in range(4):
+            w_copy(k, n, 2).wait_send()
+
+            @pl.when((z < 3) & (k <= z))
+            def _(k=k):
+                w_copy(k, n, 0).wait_send()
+
+            @pl.when((z > 0) & (k >= z))
+            def _(k=k):
+                w_copy(k, n, 1).wait_send()
+
+        return 0
+
+    lax.fori_loop(0, CHUNKS, drain, 0)
+
+
+def on_device_fused(
+    output_gradient,
+    attention_input,
+    projection_weight,
+    adapter_down,
+    adapter_up,
+    down_first_moment,
+    down_second_moment,
+    up_first_moment,
+    up_second_moment,
+    tenant_lookup,
+    active_token_rows,
+):
+    rows, width = output_gradient.shape
+    both, columns = attention_input.shape
+    rank = adapter_up.shape[1]
+    cn = columns // CHUNKS
+    piece = columns // 4
+    tall = 2 * rank + EXTRA
+    bf16, f32 = jnp.bfloat16, jnp.float32
+    dma = pltpu.SemaphoreType.DMA
+    hbm = pl.BlockSpec(memory_space=pl.ANY)
+    vmem = pl.BlockSpec(memory_space=pltpu.VMEM)
+    smem = pl.BlockSpec(memory_space=pltpu.SMEM)
+    input_gradient, sums = pl.pallas_call(
+        fused_kernel,
+        out_shape=(
+            jax.ShapeDtypeStruct((both, columns), bf16),
+            jax.ShapeDtypeStruct((4, tall, piece), f32),
+        ),
+        in_specs=[hbm, hbm, hbm, vmem, vmem, smem, smem],
+        out_specs=(hbm, hbm),
+        scratch_shapes=[
+            pltpu.VMEM((columns, width // 2), bf16),
+            pltpu.VMEM((2 * both, width // 2), bf16),
+            pltpu.VMEM((both, width // 2), bf16),
+            pltpu.VMEM((both, columns), bf16),
+            pltpu.VMEM((CHUNKS, both, cn), bf16),
+            pltpu.VMEM((4, both, cn), bf16),
+            pltpu.VMEM((4, both, cn), f32),
+            pltpu.VMEM((both, 2 * rank), f32),
+            pltpu.VMEM((both, 2 * rank), f32),
+            pltpu.VMEM((both, rank), bf16),
+            pltpu.VMEM((both, rank), bf16),
+            pltpu.VMEM((4, tall, piece), f32),
+            pltpu.VMEM((4, tall, piece), f32),
+            pltpu.VMEM((tall, piece), f32),
+            pltpu.VMEM((tall, piece), f32),
+            pltpu.VMEM((tall, piece), f32),
+            pltpu.VMEM((tall, piece), f32),
+            dma((8,)),
+            dma((4, 3, CHUNKS)),
+            dma((4, 2, CHUNKS)),
+            dma((13,)),
+            dma((13,)),
+            dma((CHUNKS,)),
+            dma((CHUNKS,)),
+            dma((CHUNKS,)),
+            dma((2,)),
+            dma((4,)),
+            dma((4,)),
+            dma((2,)),
+            dma((2,)),
+            dma((4,)),
+            dma((4,)),
+        ],
+        compiler_params=pltpu.CompilerParams(
+            collective_id=0, has_side_effects=True, vmem_limit_bytes=63 * 1024 * 1024
+        ),
+        cost_estimate=pl.CostEstimate(
+            flops=2 * both * columns * width, bytes_accessed=64 * 1024 * 1024, transcendentals=0
+        ),
+    )(
+        output_gradient,
+        attention_input,
+        projection_weight,
+        adapter_down[0].astype(bf16),
+        adapter_up[0].astype(bf16),
+        tenant_lookup,
+        active_token_rows,
+    )
+    count = sums[0, 2 * rank, 0]
+    down_gradient = sums[:, :rank, :].transpose(0, 2, 1).reshape(columns, rank) / count
+    up_gradient = sums[:, rank : 2 * rank, :].transpose(1, 0, 2).reshape(rank, columns) / count
+    fresh_down = apply_adam_rule(
+        adapter_down[0], down_gradient, down_first_moment[0], down_second_moment[0]
+    )
+    fresh_up = apply_adam_rule(adapter_up[0], up_gradient, up_first_moment[0], up_second_moment[0])
+    return (input_gradient,) + tuple(v[None] for v in fresh_down + fresh_up)
+
+
 def solution(mesh):
+    fused = mesh.shape["tensor"] == 2 and mesh.shape["dp"] == 16
     return jax.shard_map(
-        on_device,
+        on_device_fused if fused else on_device,
         mesh=mesh,
         in_specs=(
             P(("dp", "tensor"), None),

time: 667 us -> 330 us (0.49)
  waiting for transfers between devices: 534 us -> 0 us
  Pallas kernels: 0 us -> 305 us
  matrix products: 50.3 us -> 0 us
  blocking collectives: 44.4 us -> 0 us
  between operations: 16.6 us -> 1.35 us
  local copies, waits for them, and re-layouts: 2.05 us -> 13.5 us
  other arithmetic: 20 us -> 10.4 us
    all_gather x2 -> x0, waiting for transfers between devices: 398 us -> none  [the longest x1 318 us: on_device(): lax.all_gather(projection_weight, 'dp', axis=1, tiled=True)]
    pallas_call x0 -> x1, Pallas kernels: none -> 305 us  [on_device_fused(): pl.pallas_call(fused_kernel, out_shape=(jax.ShapeDtypeStruct((both, colum...]
    psum x1 -> x0, waiting for transfers between devices: 135 us -> none  [on_device(): total_a, total_b, total_count = lax.psum((slot_a, slot_b, slot_count), 'dp')]
    dot_general x6 -> x0, matrix products: 50.3 us -> none  [the longest x3 46.8 us: contract_trailing(): lax.dot_general(left, right, (((1,), (1,)), ((), ())), preferred_element_...]
    psum x2 -> x0, blocking collectives: 44.4 us -> none  [the longest x1 32.9 us: on_device(): total_a, total_b, total_count = lax.psum((slot_a, slot_b, slot_count), 'dp')]
    div x0 -> x4, local copies, waits for them, and re-layouts: none -> 7.27 us  [the longest x2 3.68 us: on_device_fused(): sums[:, rank:2 * rank, :].transpose(1, 0, 2).reshape(rank, columns) / count]
  transfers between devices with their start and end apart: 3 -> 0, of which waited for: 3 -> 0; matrix products, arithmetic and copies ran while one was open for 2% -> 0% of each run, Pallas kernels for 0% -> 0%
where the time goes in v1:
time: 330 us
  Pallas kernels  305 us (92%)
  local copies, waits for them, and re-layouts  13.5 us (4%)
  other arithmetic  10.4 us (3%)
    pallas_call x1, Pallas kernels, on_device_fused(): pl.pallas_call(fused_kernel, out_shape=(jax.ShapeDtypeStruct((both, colum...  305 us

profile of v1, /device:TPU:0, one launch (start us, length us, event | category | flops | bytes accessed | tf_op | source)
XLA Modules:
  0.0 329.9 jit_solution(474500955943501278)
XLA Ops:
  1.3 2.1 convert_bitcast_fusion.1.b_half
  3.4 2.5 copy.19
  5.9 304.6 %shard_map.162 = (bf16[384,4096]{1,0:T(8,128)(2,1)}, f32[4,136,1024]{2,1,0:T(8,128)}) custom-call(bf16[192,8192]{1,0:T(8,128)(2,1)} %g.1, bf16[384,4096]{1,0:T(8,128)(2,1)} %attn.1, bf16[4096,512]{1,0:T(8,128)(2,1)} %w.1, bf16[4096,64]{1,0:T(8,128)(2,1)} %bitcast.12, bf16[64,4096]{1,0:T(8,128)(2,1)} %convert_bitcast_fusion.1.b_half, s32[16]{0:T(128)} %lookup.1, ...), custom_call_target="tpu_custom_call" | custom-call | flops 25769803776 | bytes 67108864 | tf_op jit(solution)/shard_map/pallas_call | solution.py:569
  310.5 1.2 slice.10
  311.7 2.4 divide_bitcast_fusion
  314.1 1.6 copy.21
  315.7 0.0 copy-start
  315.7 2.0 div.89
  317.8 1.6 copy.20
  319.4 1.9 div.81
  321.4 0.0 copy-done
  321.4 0.0 copy-start.1
  321.4 0.0 copy-start.3
  321.4 0.0 copy-start.4
  321.4 3.8 %multiply_subtract_fusion.1 = (f32[1,4096,64]{1,2,0:T(8,128)}, f32[1,4096,64]{1,2,0:T(8,128)}, f32[1,4096,64]{1,2,0:T(8,128)}) fusion(f32[1,4096,64]{1,2,0:T(8,128)S(1)} %copy-done, f32[1,4096,64]{1,2,0:T(8,128)S(1)} %div.81, f32[1,4096,64]{1,2,0:T(8,128)} %param.16, f32[1,4096,64]{1,2,0:T(8,128)} %param.17), kind=kLoop, calls=%fused_computation.7 | loop fusion | flops 3407872 | bytes 7340032 | tf_op jit(solution)/shard_map/sub | solution.py:25
  325.2 0.0 copy-done.1
  325.2 0.0 copy-done.3
  325.2 0.0 copy-done.4
  325.2 0.0 copy-start.2
  325.2 2.2 multiply_subtract_fusion
  327.4 0.8 copy-done.2
  328.2 1.7 copy.24
Async XLA Ops:
  315.7 5.6 %copy-start = (f32[1,4096,64]{1,2,0:T(8,128)S(1)}, f32[1,4096,64]{1,2,0:T(8,128)}, u32[]{:S(2)}) copy-start(f32[1,4096,64]{1,2,0:T(8,128)} %param.14) | copy-start | bytes 3145732
  321.4 3.8 %copy-start.1 = (f32[1,64,4096]{2,1,0:T(8,128)S(1)}, f32[1,64,4096]{2,1,0:T(8,128)}, u32[]{:S(2)}) copy-start(f32[1,64,4096]{2,1,0:T(8,128)} %param.15) | copy-start | bytes 3145732
  321.4 3.8 %copy-start.3 = (f32[1,64,4096]{2,1,0:T(8,128)S(1)}, f32[1,64,4096]{2,1,0:T(8,128)}, u32[]{:S(2)}) copy-start(f32[1,64,4096]{2,1,0:T(8,128)} %param.18) | copy-start | bytes 3145732
  321.4 3.8 %copy-start.4 = (f32[1,64,4096]{2,1,0:T(8,128)S(1)}, f32[1,64,4096]{2,1,0:T(8,128)}, u32[]{:S(2)}) copy-start(f32[1,64,4096]{2,1,0:T(8,128)} %param.19) | copy-start | bytes 3145732
  325.2 3.0 copy-start.2
